TPU v7x, 32 devices: a whole 2x2x4 slice. The times are simulated.
32 devices in a mesh: row: 4 (over y, x), col: 8 (over z, core).
Axes of the slice: x: 2, y: 2, z: 4, core: 2. Of those that a mesh axis runs over, the one named last changes fastest.
Arguments:
- z_slab: float32 [1024, 1024], P('col', 'row'), may hold values from -6 to 6
- prev_factor: bfloat16 [1024, 32768], P('row', 'col'), may hold values from -0.03125 to 0.03125
- prev_solution: bfloat16 [1024, 32768], P(None, 'col'), may hold values from -6 to 6
- slab_factor: bfloat16 [1024, 1024], P('row'), may hold values from -0.09375 to 0.09375
- diag_inverse: bfloat16 [1024, 256], P('row'), may hold values from -1 to 2, as said below
Outputs:
- solved: float32 [1024, 1024], P('col', 'row')
Inputs may be any that keep to these rules, and one draw needn't show every extreme that they name: `diag_inverse`: each 256 x 256 block is lower triangular with its diagonal between 1 and 2.
All inputs are finite; a program needn't handle non-finite values.
Results may differ from a plain program's by a relative error of at most 0.0003.
Values sent between devices are 32-bit elements; how exact they have to be, the bound alone decides.
A program may use at most 64 MiB of HBM per device.

v0:
```python
import jax
import jax.numpy as jnp
from jax import lax
from jax.sharding import PartitionSpec as P


def spread(block, axis, owner):
    block = jnp.where(lax.axis_index(axis) == owner, block, jnp.zeros_like(block))
    return lax.psum(block, axis)


def precise_dot(left, right):
    return lax.dot_general(
        left,
        right,
        (((1,), (1,)), ((), ())),
        precision=lax.Precision.HIGHEST,
        preferred_element_type=jnp.float32,
    )


def on_device(z_slab, prev_factor, prev_solution, slab_factor, diag_inverse):
    row_count = z_slab.shape[0]
    block_width = diag_inverse.shape[1]
    block_rows = lax.axis_size("row")
    partial_value = lax.dot_general(
        prev_solution, prev_factor, (((1,), (1,)), ((), ())), preferred_element_type=jnp.float32
    )
    summed = lax.psum(partial_value, "col")
    fan_sum = lax.dynamic_slice_in_dim(summed, lax.axis_index("col") * row_count, row_count, 0)
    remainder = z_slab - fan_sum
    factor = slab_factor.astype(jnp.float32)
    inverse = diag_inverse.astype(jnp.float32)
    device_row = lax.axis_index("row")
    result = jnp.zeros((row_count, block_width), jnp.float32)
    updates = jnp.zeros((row_count, block_width), jnp.float32)

    def bcast_step(block_index, carry):
        result, updates = carry
        candidate = precise_dot(remainder - updates, inverse)
        arrived = spread(candidate, "row", block_index)
        result = jnp.where(device_row == block_index, arrived, result)
        columns = lax.dynamic_slice_in_dim(factor, block_index * block_width, block_width, 1)
        updates = updates + precise_dot(arrived, columns)
        return (result, updates)

    result, updates = lax.fori_loop(0, block_rows, bcast_step, (result, updates))
    return result


def solution(mesh):
    in_specs = (P("col", "row"), P("row", "col"), P(None, "col"), P("row", None), P("row", None))
    out_specs = P("col", "row")
    return jax.shard_map(
        on_device, mesh=mesh, in_specs=in_specs, out_specs=out_specs, check_vma=False
    )
```

profile of v0, /device:TPU:0, one launch (start us, length us, event | category | flops | bytes accessed | tf_op | source)
XLA Modules:
  0.0 277.1 jit_solution(165684188814202454)
XLA Ops:
  6.5 1.6 copy-done
  8.1 6.8 %fusion.7 = f32[1024,256]{1,0:T(8,128)} fusion(bf16[1024,4096]{1,0:T(8,128)(2,1)} %param.9, bf16[256,4096]{1,0:T(8,128)(2,1)S(1)} %copy-done), kind=kOutput, calls=%fused_computation.11 | convolution fusion | flops 2147483648 | bytes 11534336 | tf_op jit(solution)/shard_map/dot_general | solution.py:26
  14.9 0.0 all-reduce.3.cloned.1.call-update
  14.9 1.1 convert_element_type.7
  16.1 0.9 convert_element_type.6
  17.0 59.6 %all-reduce.3.cloned.1.call-done = f32[1024,256]{1,0:T(8,128)} async-done(((f32[1024,256]{1,0:T(8,128)}), f32[1024,256]{1,0:T(8,128)}) %all-reduce.3.cloned.1.call-update) | async-done | bytes 1048592 | tf_op jit(solution)/shard_map/psum | solution.py:29
  76.6 1.6 dynamic-slice_subtract_fusion
  78.3 192.3 %while.16 = (s32[]{:T(128)}, f32[128,256]{1,0:T(8,128)}, f32[128,256]{1,0:T(8,128)S(1)}, s32[]{:T(128)}, f32[128,256]{1,0:T(8,128)}, /*index=5*/f32[256,256]{1,0...) while((s32[]{:T(128)}, f32[128,256]{1,0:T(8,128)}, ...), condition=%wide.region_3.4_spmd.clone, body=%wide.region_1.3_spmd.clone.sunk | while | flops 201588736 | bytes 2490639 | solution.py:47
  78.3 1.9 convolution_select_fusion.2
  80.3 42.7 %all-reduce.5.cloned.1.call-done = f32[128,256]{1,0:T(8,128)} async-done(((f32[128,256]{1,0:T(8,128)}), f32[128,256]{1,0:T(8,128)}) %all-reduce.5.cloned.1.call-update) | async-done | bytes 131088 | tf_op jit(solution)/shard_map/while/body/eval_jaxpr/psum | solution.py:9
  123.0 1.4 convolution_add_fusion.2
  124.3 1.6 select_select_fusion.2
  125.9 2.0 convolution_select_fusion.2
  127.9 42.9 %all-reduce.5.cloned.1.call-done = f32[128,256]{1,0:T(8,128)} async-done(((f32[128,256]{1,0:T(8,128)}), f32[128,256]{1,0:T(8,128)}) %all-reduce.5.cloned.1.call-update) | async-done | bytes 131088 | tf_op jit(solution)/shard_map/while/body/eval_jaxpr/psum | solution.py:9
  170.8 1.4 convolution_add_fusion.2
  172.1 1.6 select_select_fusion.2
  173.7 1.9 convolution_select_fusion.2
  175.7 43.5 %all-reduce.5.cloned.1.call-done = f32[128,256]{1,0:T(8,128)} async-done(((f32[128,256]{1,0:T(8,128)}), f32[128,256]{1,0:T(8,128)}) %all-reduce.5.cloned.1.call-update) | async-done | bytes 131088 | tf_op jit(solution)/shard_map/while/body/eval_jaxpr/psum | solution.py:9
  219.2 1.4 convolution_add_fusion.2
  220.6 1.6 select_select_fusion.2
  222.2 1.9 convolution_select_fusion.2
  224.2 43.4 %all-reduce.5.cloned.1.call-done = f32[128,256]{1,0:T(8,128)} async-done(((f32[128,256]{1,0:T(8,128)}), f32[128,256]{1,0:T(8,128)}) %all-reduce.5.cloned.1.call-update) | async-done | bytes 131088 | tf_op jit(solution)/shard_map/while/body/eval_jaxpr/psum | solution.py:9
  267.6 1.4 convolution_add_fusion.2
  269.0 1.6 select_select_fusion.2
  (12 shorter events, 0.1 us)
Async XLA Ops:
  6.5 1.6 copy-start
  6.5 70.1 %all-reduce.3.cloned.1.call-start = ((), (), s32[]{:S(2)}) async-start(), calls=%async_computation | async-start | bytes 2097152 | tf_op jit(solution)/shard_map/psum | solution.py:29
  78.3 44.7 %all-reduce.5.cloned.1.call-start = ((), (), s32[]{:S(2)}) async-start(), calls=%async_computation.1 | async-start | bytes 262144 | tf_op jit(solution)/shard_map/while/body/eval_jaxpr/psum | solution.py:9
  125.9 44.9 %all-reduce.5.cloned.1.call-start = ((), (), s32[]{:S(2)}) async-start(), calls=%async_computation.1 | async-start | bytes 262144 | tf_op jit(solution)/shard_map/while/body/eval_jaxpr/psum | solution.py:9
  173.7 45.5 %all-reduce.5.cloned.1.call-start = ((), (), s32[]{:S(2)}) async-start(), calls=%async_computation.1 | async-start | bytes 262144 | tf_op jit(solution)/shard_map/while/body/eval_jaxpr/psum | solution.py:9
  222.2 45.4 %all-reduce.5.cloned.1.call-start = ((), (), s32[]{:S(2)}) async-start(), calls=%async_computation.1 | async-start | bytes 262144 | tf_op jit(solution)/shard_map/while/body/eval_jaxpr/psum | solution.py:9
Sparse Core Ops, SparseCore 0:
  15.0 61.5 all-reduce.2
  82.0 40.9 all-reduce.4
  129.6 41.1 all-reduce.4
  177.1 42.0 all-reduce.4
  225.6 41.9 all-reduce.4
where the time goes:
time: 278 us; the launch traced here: 277 us
  waiting for transfers between devices  232 us (83%)
  matrix products  20 us (7%)
  between operations  13.1 us (5%)
  other arithmetic  10.1 us (4%)
    psum x4, waiting for transfers between devices, spread(): return lax.psum(block, axis)  173 us
    psum x1, waiting for transfers between devices, on_device(): summed = lax.psum(partial_value, 'col')  59.6 us
    dot_general x8, matrix products, precise_dot(): lax.dot_general(left, right, (((1,), (1,)), ((), ())), precision=lax.Prec...  13.2 us
    dot_general x1, matrix products, on_device(): lax.dot_general(prev_solution, prev_factor, (((1,), (1,)), ((), ())), pre...  6.76 us
    select_n x4, other arithmetic, bcast_step(): result = jnp.where(device_row == block_index, arrived, result)  6.36 us
  transfers between devices with their start and end apart: 5, of which 5 were waited for; matrix products, arithmetic and copies ran while one was open for 1% of the time, Pallas kernels for 0%

commit v1 on v0

--- a/solution.py
+++ b/solution.py
@@ -2,11 +2,13 @@
 import jax.numpy as jnp
 from jax import lax
 from jax.sharding import PartitionSpec as P
+from jax.lax import all_gather
 
 
 def spread(block, axis, owner):
     block = jnp.where(lax.axis_index(axis) == owner, block, jnp.zeros_like(block))
-    return lax.psum(block, axis)
+    fix_hubs = lambda local, chip_axis: all_gather(local, axis_name=chip_axis).sum(axis=0)
+    return fix_hubs(block, chip_axis=axis)
 
 
 def precise_dot(left, right):

time: 278 us -> 133 us (0.48)
  waiting for transfers between devices: 232 us -> 60.6 us
  blocking collectives: 0 us -> 39.7 us
  other arithmetic: 10.1 us -> 2.31 us
  matrix products: 20 us -> 14 us
    psum x4 -> x0, waiting for transfers between devices: 173 us -> none  [spread(): return lax.psum(block, axis)]
    all_gather x0 -> x4, blocking collectives: none -> 39.7 us  [spread(): all_gather(local, axis_name=chip_axis).sum(axis=0)]
    select_n x4, other arithmetic: 6.36 us -> 0.14 us  [bcast_step(): result = jnp.where(device_row == block_index, arrived, result)]
    dot_general x8, matrix products: 13.2 us -> 7.24 us  [precise_dot(): lax.dot_general(left, right, (((1,), (1,)), ((), ())), precision=lax.Prec...]
  transfers between devices with their start and end apart: 5 -> 1, of which waited for: 5 -> 1; matrix products, arithmetic and copies ran while one was open for 1% -> 1% of each run, Pallas kernels for 0% -> 0%
where the time goes in v1:
time: 133 us
  waiting for transfers between devices  60.6 us (46%)
  blocking collectives  39.7 us (30%)
  matrix products  14 us (11%)
  between operations  13.5 us (10%)
  other arithmetic  2.31 us (2%)
  local copies, waits for them, and re-layouts  2.2 us (2%)
    psum x1, waiting for transfers between devices, on_device(): summed = lax.psum(partial_value, 'col')  60.6 us
    all_gather x4, blocking collectives, spread(): all_gather(local, axis_name=chip_axis).sum(axis=0)  39.7 us
    dot_general x8, matrix products, precise_dot(): lax.dot_general(left, right, (((1,), (1,)), ((), ())), precision=lax.Prec...  7.24 us
    dot_general x1, matrix products, on_device(): lax.dot_general(prev_solution, prev_factor, (((1,), (1,)), ((), ())), pre...  6.74 us
  transfers between devices with their start and end apart: 1, of which 1 were waited for; matrix products, arithmetic and copies ran while one was open for 1% of the time, Pallas kernels for 0%

profile of v1, /device:TPU:0, one launch (start us, length us, event | category | flops | bytes accessed | tf_op | source)
XLA Modules:
  0.0 132.5 jit_solution(3107362448296787316)
XLA Ops:
  6.5 0.0 copy-start
  6.5 0.0 all-reduce.2.cloned.1.call-start
  6.6 1.5 %copy-done = bf16[256,4096]{1,0:T(8,128)(2,1)S(1)} copy-done((bf16[256,4096]{1,0:T(8,128)(2,1)S(1)}, bf16[256,4096]{1,0:T(8,128)(2,1)}, u32[]{:S(2)}) %copy-start) | copy-done | bytes 2097176
  8.1 6.7 %fusion.7 = f32[1024,256]{1,0:T(8,128)} fusion(bf16[1024,4096]{1,0:T(8,128)(2,1)} %param.9, bf16[256,4096]{1,0:T(8,128)(2,1)S(1)} %copy-done), kind=kOutput, calls=%fused_computation.11 | convolution fusion | flops 2147483648 | bytes 11534336 | tf_op jit(solution)/shard_map/dot_general | solution.py:28
  14.9 0.0 all-reduce.2.cloned.1.call-update
  14.9 1.1 convert_element_type.7
  16.0 60.6 %all-reduce.2.cloned.1.call-done = f32[1024,256]{1,0:T(8,128)} async-done(((f32[1024,256]{1,0:T(8,128)}), f32[1024,256]{1,0:T(8,128)}) %all-reduce.2.cloned.1.call-update) | async-done | bytes 1048592 | tf_op jit(solution)/shard_map/psum | solution.py:31
  76.6 0.0 copy-done.4
  76.6 0.9 dynamic-slice_subtract_fusion
  77.5 47.5 %while.16 = (s32[]{:T(128)}, f32[128,256]{1,0:T(8,128)S(1)}, f32[128,256]{1,0:T(8,128)S(1)}, s32[]{:T(128)}, f32[128,256]{1,0:T(8,128)S(1)}, /*index=5*/f32[256,...) while((s32[]{:T(128)}, f32[128,256]{1,0:T(8,128)S(1)}, ...), condition=%wide.region_3.4_spmd.clone, body=%wide.region_1.3_spmd.clone.sunk | while | flops 201654272 | bytes 3014899 | solution.py:49
  77.6 0.4 convolution_select_fusion.2
  78.0 10.7 %all-gather.3 = f32[512,256]{1,0:T(8,128)S(1)} all-gather(f32[128,256]{1,0:T(8,128)S(1)} %convolution_select_fusion.2), channel_id=2, replica_groups=mesh['row'=4,'col'=8] {'row'}, dimensions={0}, use_global_device_ids=true | all-gather | bytes 655360 | tf_op jit(solution)/shard_map/while/body/eval_jaxpr/all_gather | solution.py:10
  88.7 1.4 %convolution_add_fusion.2 = f32[128,256]{1,0:T(8,128)S(1)} fusion(f32[128,256]{1,0:T(8,128)S(1)} %reduce_sum.15, f32[256,1024]{1,0:T(8,128)} %get-tuple-element.243, s32[]{:T(128)S(6)} %select_n.59, f32[128,256]{1,0:T(8,128)S(1)} %get-tuple-element.226, pred[]{:T(512)S(6)} %compare.3), kind=kOutput, calls=%fused_computation.clone.1 | convolution fusion | flops 100728832 | bytes 655365 | tf_op jit(solution)/shard_map/while/body/eval_jaxpr/dot_general | solution.py:15
  90.2 0.4 convolution_select_fusion.2
  90.6 9.7 %all-gather.3 = f32[512,256]{1,0:T(8,128)S(1)} all-gather(f32[128,256]{1,0:T(8,128)S(1)} %convolution_select_fusion.2), channel_id=2, replica_groups=mesh['row'=4,'col'=8] {'row'}, dimensions={0}, use_global_device_ids=true | all-gather | bytes 655360 | tf_op jit(solution)/shard_map/while/body/eval_jaxpr/all_gather | solution.py:10
  100.3 1.4 %convolution_add_fusion.2 = f32[128,256]{1,0:T(8,128)S(1)} fusion(f32[128,256]{1,0:T(8,128)S(1)} %reduce_sum.15, f32[256,1024]{1,0:T(8,128)} %get-tuple-element.243, s32[]{:T(128)S(6)} %select_n.59, f32[128,256]{1,0:T(8,128)S(1)} %get-tuple-element.226, pred[]{:T(512)S(6)} %compare.3), kind=kOutput, calls=%fused_computation.clone.1 | convolution fusion | flops 100728832 | bytes 655365 | tf_op jit(solution)/shard_map/while/body/eval_jaxpr/dot_general | solution.py:15
  101.8 0.4 convolution_select_fusion.2
  102.2 9.6 %all-gather.3 = f32[512,256]{1,0:T(8,128)S(1)} all-gather(f32[128,256]{1,0:T(8,128)S(1)} %convolution_select_fusion.2), channel_id=2, replica_groups=mesh['row'=4,'col'=8] {'row'}, dimensions={0}, use_global_device_ids=true | all-gather | bytes 655360 | tf_op jit(solution)/shard_map/while/body/eval_jaxpr/all_gather | solution.py:10
  111.8 1.4 %convolution_add_fusion.2 = f32[128,256]{1,0:T(8,128)S(1)} fusion(f32[128,256]{1,0:T(8,128)S(1)} %reduce_sum.15, f32[256,1024]{1,0:T(8,128)} %get-tuple-element.243, s32[]{:T(128)S(6)} %select_n.59, f32[128,256]{1,0:T(8,128)S(1)} %get-tuple-element.226, pred[]{:T(512)S(6)} %compare.3), kind=kOutput, calls=%fused_computation.clone.1 | convolution fusion | flops 100728832 | bytes 655365 | tf_op jit(solution)/shard_map/while/body/eval_jaxpr/dot_general | solution.py:15
  113.3 0.4 convolution_select_fusion.2
  113.7 9.7 %all-gather.3 = f32[512,256]{1,0:T(8,128)S(1)} all-gather(f32[128,256]{1,0:T(8,128)S(1)} %convolution_select_fusion.2), channel_id=2, replica_groups=mesh['row'=4,'col'=8] {'row'}, dimensions={0}, use_global_device_ids=true | all-gather | bytes 655360 | tf_op jit(solution)/shard_map/while/body/eval_jaxpr/all_gather | solution.py:10
  123.5 1.4 %convolution_add_fusion.2 = f32[128,256]{1,0:T(8,128)S(1)} fusion(f32[128,256]{1,0:T(8,128)S(1)} %reduce_sum.15, f32[256,1024]{1,0:T(8,128)} %get-tuple-element.243, s32[]{:T(128)S(6)} %select_n.59, f32[128,256]{1,0:T(8,128)S(1)} %get-tuple-element.226, pred[]{:T(512)S(6)} %compare.3), kind=kOutput, calls=%fused_computation.clone.1 | convolution fusion | flops 100728832 | bytes 655365 | tf_op jit(solution)/shard_map/while/body/eval_jaxpr/dot_general | solution.py:15
  125.0 0.0 copy-start.1
  125.0 0.6 copy-done.1
  (16 shorter events, 0.3 us)
Async XLA Ops:
  6.5 1.6 %copy-start = (bf16[256,4096]{1,0:T(8,128)(2,1)S(1)}, bf16[256,4096]{1,0:T(8,128)(2,1)}, u32[]{:S(2)}) copy-start(bf16[256,4096]{1,0:T(8,128)(2,1)} %param.8) | copy-start | bytes 6291460
  6.5 8.4 %copy-start.2 = (bf16[256,1024]{1,0:T(8,128)(2,1)S(1)}, bf16[256,1024]{1,0:T(8,128)(2,1)}, u32[]{:S(2)}) copy-start(bf16[256,1024]{1,0:T(8,128)(2,1)} %param.10) | copy-start | bytes 1572868
  6.5 9.5 %copy-start.3 = (bf16[256,256]{1,0:T(8,128)(2,1)S(1)}, bf16[256,256]{1,0:T(8,128)(2,1)}, u32[]{:S(2)}) copy-start(bf16[256,256]{1,0:T(8,128)(2,1)} %param.11) | copy-start | bytes 393220
  6.5 70.1 %copy-start.4 = (f32[128,256]{1,0:T(8,128)S(1)}, f32[128,256]{1,0:T(8,128)}, u32[]{:S(2)}) copy-start(f32[128,256]{1,0:T(8,128)} %param.7) | copy-start | bytes 393220
  6.5 70.1 %all-reduce.2.cloned.1.call-start = ((), (), s32[]{:S(2)}) async-start(), calls=%async_computation | async-start | bytes 2097152 | tf_op jit(solution)/shard_map/psum | solution.py:31
  125.0 0.7 copy-start.1
Sparse Core Ops, SparseCore 0:
  15.0 61.5 all-reduce.1
